TPU v7x, 32 devices: a whole 2x2x4 slice. The times are simulated.
32 devices in a mesh: stn: 2 (over y), tm: 8 (over z, core), cores: 2 (over x).
Axes of the slice: x: 2, y: 2, z: 4, core: 2. Of those that a mesh axis runs over, the one named last changes fastest.
Arguments:
- samples: bfloat16 [64, 2097152], P('stn', ('tm', 'cores')), may hold values from -6 to 6
- delays: int32 [64], P('stn'), may hold values from 0 to 32768, as said below
- valid: int32 [64], P('stn'), may hold values 0 or 1
- tone_chan: int32 [64, 64], P('stn'), may hold values from 0 to 16383
Outputs:
- visibility: float32 [16384, 8192], P(('stn', 'tm', 'cores'))
- phase_cal: float32 [64, 128], P('stn')
Inputs may be any that keep to these rules, and one draw needn't show every extreme that they name: `delays`: each station's delay in samples; some station has a delay of exactly 32768.
All inputs are finite; a program needn't handle non-finite values. No bound on the sum of `valid` on one device may be relied on, other than what follows from the above.
Results may differ from a plain program's by a relative error of at most 0.007.
Values may be sent and summed in bfloat16 or wider, within the bound.
A program may use at most 128 MiB of HBM per device.

v0:
```python
import math

import jax
import jax.numpy as jnp
import ml_dtypes
import numpy as np
from jax import lax
from jax.experimental import pallas as pl
from jax.experimental.pallas import tpu as pltpu
from jax.sharding import PartitionSpec as P

S = 64
NCH = 16384
FA = 256
FB = 128
NTONE = 64
MAXD = 32768


def passed_along(block, axis, distance):
    devices = range(lax.axis_size(axis))
    route = [(i - distance, i) for i in devices if i - distance in devices]
    return lax.ppermute(block, axis, route)


def make_tables():
    outer_idx = jnp.arange(FA, dtype=jnp.int32)
    phases = outer_idx[:, None] * outer_idx[None, :] % FA
    angles = 2.0 * math.pi / FA * phases.astype(jnp.float32)
    section_one = jnp.stack([jnp.cos(angles), -jnp.sin(angles)]).astype(jnp.bfloat16)
    inner_idx = jnp.arange(FB, dtype=jnp.int32)
    spectrum_len = FA * FB
    twist_idx = outer_idx[:, None] * inner_idx[None, :] % spectrum_len
    twists = 2.0 * math.pi / spectrum_len * twist_idx.astype(jnp.float32)
    norm_scale = 1.0 / math.sqrt(spectrum_len)
    twist_cos = jnp.cos(twists) * norm_scale
    twist_sin = jnp.sin(twists) * norm_scale
    half_idx = jnp.arange(FB // 2, dtype=jnp.int32)
    last_idx = inner_idx[:, None] * half_idx[None, :] % FB
    thetas = 2.0 * math.pi / FB * last_idx.astype(jnp.float32)
    cosine = jnp.cos(thetas)
    sine_val = jnp.sin(thetas)
    section_two = jnp.stack(
        [jnp.stack([cosine, -sine_val], axis=1), jnp.stack([sine_val, cosine], axis=1)]
    ).astype(jnp.bfloat16)
    return (section_one, twist_cos, twist_sin, section_two)


def channelize(window, usable, tables):
    section_one, twist_cos, twist_sin, section_two = tables
    spec_count = window.shape[0] // (FA * FB)
    blocks = window.reshape(spec_count, FA, FB)
    section_out = jnp.einsum(
        "xkn,bnm->bxkm", section_one, blocks, preferred_element_type=jnp.float32
    )
    real_part = section_out[:, 0] * twist_cos + section_out[:, 1] * twist_sin
    imag_part = section_out[:, 1] * twist_cos - section_out[:, 0] * twist_sin
    twisted = jnp.stack([real_part, imag_part], axis=1).astype(jnp.bfloat16)
    product = jnp.einsum(
        "xnrq,bxkn->brqk", section_two, twisted, preferred_element_type=jnp.float32
    )
    return (product.reshape(spec_count, 2, NCH) * usable).astype(jnp.bfloat16)


def cross_power(matrix):
    gram = jnp.einsum("cta,ctb->cab", matrix, matrix, preferred_element_type=jnp.float32)
    real_re = gram[:, :S, :S]
    imag_im = gram[:, S:, S:]
    imag_re = gram[:, S:, :S]
    real_im = gram[:, :S, S:]
    channels = gram.shape[0]
    first = (real_re + imag_im).reshape(channels, S * S)
    second = (imag_re - real_im).reshape(channels, S * S)
    return jnp.concatenate([first, second], axis=1)


def shards(samples, delays, valid, tone_chan):
    tables = make_tables()
    stretch = samples.shape[1]
    spectrum_len = FA * FB
    trailing = passed_along(samples[:, :MAXD], ("tm", "cores"), -1)
    extended = jnp.concatenate([samples, trailing], axis=1)
    chan_ids = jnp.arange(NCH, dtype=jnp.int32)

    def station(inputs):
        stream, shift_by, usable, tone_ids = inputs
        window = lax.dynamic_slice_in_dim(stream, shift_by, stretch)
        spectra = channelize(window, usable.astype(jnp.float32), tables)
        totals = jnp.sum(spectra, axis=0, dtype=jnp.float32)
        selector = (chan_ids[:, None] == tone_ids[None, :]).astype(jnp.float32)
        picked = jnp.dot(
            totals, selector, precision=lax.Precision.HIGHEST, preferred_element_type=jnp.float32
        )
        return (spectra, picked.reshape(2 * NTONE))

    spectra, tone_picks = lax.map(station, (extended, delays, valid, tone_chan))
    spectra_all = stretch // spectrum_len * lax.axis_size("tm") * lax.axis_size("cores")
    norm_scale = 1.0 / math.sqrt(spectra_all)
    phase_cal = lax.psum(tone_picks, ("tm", "cores")) * norm_scale
    local_stn = spectra.shape[0]
    spec_here = spectra.shape[1]
    n_stn = lax.axis_size("stn")
    n_tm = lax.axis_size("tm")
    received = lax.all_to_all(spectra[None], ("stn", "tm"), split_axis=4, concat_axis=0, tiled=True)
    block_in = received.shape[4]
    arranged = received.reshape(n_stn, n_tm, local_stn, spec_here, 2, block_in)
    turned = jnp.transpose(arranged, (0, 2, 1, 3, 4, 5)).reshape(
        n_stn * local_stn, n_tm * spec_here, 2, block_in
    )
    block = turned.shape[3]
    halves = turned.reshape(turned.shape[0], turned.shape[1], 2, 2, block // 2)
    halves = lax.all_to_all(halves, "cores", split_axis=3, concat_axis=1, tiled=True)
    turned = halves.reshape(halves.shape[0], halves.shape[1], 2, block // 2)
    rows = turned.shape[1]
    matrix = jnp.transpose(turned, (3, 1, 2, 0)).reshape(turned.shape[3], rows, 2 * S)
    partial_value = cross_power(matrix)
    return (partial_value * norm_scale, phase_cal)


LANES = 128
VMEM_LIMIT = 56 * 1024 * 1024


def fast_tables():
    def turn(left, right, period):
        angle = np.float32(2.0 * math.pi / period)
        phases = (np.arange(left)[:, None] * np.arange(right)[None, :] % period).astype(np.float32)
        return np.cos(angle * phases), np.sin(angle * phases)

    cosine, sine = turn(FA, FA, FA)
    first = np.concatenate([cosine, -sine], axis=0).astype(ml_dtypes.bfloat16)
    cosine, sine = turn(FA, FB, FA * FB)
    norm_scale = np.float32(1.0 / math.sqrt(FA * FB))
    twist_cos, twist_sin = cosine * norm_scale, sine * norm_scale
    cosine, sine = turn(FB // 2, FB, FB)
    last = np.concatenate([cosine, sine], axis=1).astype(ml_dtypes.bfloat16)
    return tuple(jnp.asarray(table) for table in (first, twist_cos, twist_sin, last))


def first_stage(s, delay, usable, one_ref, cos_ref, sin_ref, stream, twist_re, twist_im):
    rows = 2 * FA
    whole = delay // LANES
    part = delay % LANES
    lane = lax.broadcasted_iota(jnp.int32, (rows, LANES), 1)
    here = stream[pl.ds(whole, rows), :]
    after = stream[pl.ds(whole + 1, rows), :]
    mixed = jnp.where(lane < part, after, here)
    shifted = pltpu.roll(mixed, (LANES - part) % LANES, 1).astype(jnp.bfloat16)
    both = jnp.concatenate([shifted[:FA], shifted[FA:]], axis=1)
    section = jnp.dot(one_ref[...], both, preferred_element_type=jnp.float32)
    cosine = cos_ref[...] * usable
    sine = sin_ref[...] * usable
    for t in range(2):
        re = section[:FA, t * LANES : (t + 1) * LANES]
        im = section[FA:, t * LANES : (t + 1) * LANES]
        twist_re[pl.ds(t * 32 + s, FA, stride=PITCH), :] = re * cosine + im * sine
        twist_im[pl.ds(t * 32 + s, FA, stride=PITCH), :] = im * cosine - re * sine


def second_stage(two_ref, out_ref, twist_re, twist_im, turned):
    def second(k, carry):
        re = twist_re[pl.ds(k * PITCH, 64), :].astype(jnp.bfloat16)
        im = twist_im[pl.ds(k * PITCH, 64), :].astype(jnp.bfloat16)
        right = jnp.concatenate(
            [jnp.concatenate([re, im], axis=1), jnp.concatenate([im, -re], axis=1)], axis=0
        )
        product = lax.dot_general(
            two_ref[...], right, (((1,), (1,)), ((), ())), preferred_element_type=jnp.float32
        )
        turned[pl.ds(k, FB // 2, stride=FA + 1), :] = product
        return carry

    lax.fori_loop(0, FA, second, 0, unroll=8)

    def write(q, carry):
        out_ref[q] = turned[pl.ds(q * (FA + 1), FA), :].astype(jnp.bfloat16)
        return carry

    lax.fori_loop(0, FB // 2, write, 0, unroll=2)


PITCH = 65
STAGE_SCRATCH = [
    pltpu.VMEM((3 * FA + 8, LANES), jnp.float32),
    pltpu.VMEM((FA * PITCH + 7, LANES), jnp.float32),
    pltpu.VMEM((FA * PITCH + 7, LANES), jnp.float32),
    pltpu.VMEM(((FA + 1) * FB // 2, LANES), jnp.float32),
]


def channelize_kernel(delay_ref, valid_ref, main_ref, next_ref, one_ref, cos_ref, sin_ref, two_ref,
                      out_ref, stream, twist_re, twist_im, turned):
    s = pl.program_id(0)
    rows = 2 * FA
    stream[0:rows, :] = main_ref[0].astype(jnp.float32)
    stream[rows : rows + FA, :] = next_ref[0].astype(jnp.float32)
    first_stage(s, delay_ref[s], valid_ref[s].astype(jnp.float32), one_ref, cos_ref, sin_ref,
                stream, twist_re, twist_im)

    @pl.when(s == pl.num_programs(0) - 1)
    def _():
        second_stage(two_ref, out_ref, twist_re, twist_im, turned)


def channelize_pair(pair, blocks, following, delays, valid, tables):
    first, twist_cos, twist_sin, last = tables
    source, next_at = following
    whole = lambda shape: pl.BlockSpec(shape, lambda s, *_: (0,) * len(shape))
    return pl.pallas_call(
        channelize_kernel,
        out_shape=jax.ShapeDtypeStruct((FB // 2, FA, LANES), jnp.bfloat16),
        grid_spec=pltpu.PrefetchScalarGridSpec(
            num_scalar_prefetch=2,
            grid=(blocks.shape[0],),
            in_specs=[
                pl.BlockSpec((1, 2 * FA, LANES), lambda s, *_: (s, pair, 0)),
                pl.BlockSpec((1, FA, LANES), lambda s, *_: (s, next_at, 0)),
                whole((2 * FA, FA)),
                whole((FA, FB)),
                whole((FA, FB)),
                whole((FB // 2, 2 * FB)),
            ],
            out_specs=whole((FB // 2, FA, LANES)),
            scratch_shapes=STAGE_SCRATCH,
        ),
        compiler_params=pltpu.CompilerParams(vmem_limit_bytes=VMEM_LIMIT),
        cost_estimate=pl.CostEstimate(
            flops=3 * 2 * 64 * 256 * 256 * 256, bytes_accessed=10 * 2**20, transcendentals=0
        ),
    )(delays, valid, blocks, source, first, twist_cos, twist_sin, last)


def linear_index(sizes):
    n_stn, n_tm, n_cores = sizes
    return (lax.axis_index("stn") * n_tm + lax.axis_index("tm")) * n_cores + lax.axis_index("cores")


def pick_tones(tone_ref, turned, picks, stations, first):
    lane = lax.broadcasted_iota(jnp.int32, (1, LANES), 1) % 32

    def tone(k, carry):
        row = jnp.zeros((1, LANES), jnp.float32)
        for s in range(stations):
            channel = tone_ref[s, k]
            row = jnp.where(lane == s, turned[pl.ds(channel + channel // FA, 1), :], row)
        row = row.astype(jnp.bfloat16).astype(jnp.float32)
        picks[pl.ds(k, 1), :] = row if first else picks[pl.ds(k, 1), :] + row
        return carry

    lax.fori_loop(0, NTONE, tone, 0)


def exchange_kernel(sizes, scale, zero_ref, delay_ref, valid_ref, tone_ref, main_ref, next_ref, one_ref,
                    cos_ref, sin_ref, two_ref, got_ref, tones_ref, stream, twist_re, twist_im,
                    turned, later, picks, sent, arrived, local_sem, send_sem, recv_sem, load_sem,
                    tone_send, tone_recv):
    _, n_tm, n_cores = sizes
    n = math.prod(sizes)
    me = linear_index(sizes)

    def place(device):
        return (device // (n_tm * n_cores), (device // n_cores) % n_tm, device % n_cores)

    barrier = pltpu.get_barrier_semaphore()

    def greet(k, carry):
        pl.semaphore_signal(
            barrier, inc=1, device_id=place((me + k) % n), device_id_type=pl.DeviceIdType.MESH
        )
        return carry

    lax.fori_loop(1, n, greet, 0)
    pl.semaphore_wait(barrier, n - 1)
    sources = (zero_ref, later)

    def copy(pair, k):
        to = (me + k) % n
        return pltpu.make_async_remote_copy(
            src_ref=sources[pair].at[pl.ds(to * 2, 2)],
            dst_ref=got_ref.at[pair, me],
            send_sem=send_sem.at[pair, k],
            recv_sem=recv_sem.at[pair, k],
            device_id=place(to),
            device_id_type=pl.DeviceIdType.MESH,
        )

    def own(pair):
        return pltpu.make_async_copy(
            sources[pair].at[pl.ds(me * 2, 2)], got_ref.at[pair, me], local_sem.at[pair]
        )

    def send(pair):
        lax.fori_loop(1, n, lambda k, carry: (copy(pair, k).start(), carry)[1], 0)
        own(pair).start()

    def finish(pair):
        own(pair).wait()
        lax.fori_loop(1, n, lambda k, carry: (copy(pair, k).wait(), carry)[1], 0)

    send(0)
    load = pltpu.make_async_copy(zero_ref, later, load_sem)
    load.start()
    load.wait()

    def widen(q, carry):
        turned[pl.ds(q * (FA + 1), FA), :] = later[q].astype(jnp.float32)
        return carry

    lax.fori_loop(0, FB // 2, widen, 0, unroll=2)
    stations = main_ref.shape[0]
    pick_tones(tone_ref, turned, picks, stations, True)

    def station(s, carry):
        rows = 2 * FA
        stream[0:rows, :] = main_ref[s].astype(jnp.float32)
        stream[rows : rows + FA, :] = next_ref[s].astype(jnp.float32)
        first_stage(s, delay_ref[s], valid_ref[s].astype(jnp.float32), one_ref, cos_ref, sin_ref,
                    stream, twist_re, twist_im)
        return carry

    lax.fori_loop(0, stations, station, 0)
    second_stage(two_ref, later, twist_re, twist_im, turned)
    send(1)
    pick_tones(tone_ref, turned, picks, stations, False)
    running = picks[...] + pltpu.roll(picks[...], 96, 1)
    flips = []
    for name, size in (("cores", n_cores), ("tm", n_tm)):
        bit = 1
        while bit < size:
            at = lax.axis_index(name)
            flips.append({name: at + bit * (1 - 2 * ((at // bit) % 2))})
            bit *= 2
    for r, partner in enumerate(flips):
        sent[r] = running
        passing = pltpu.make_async_remote_copy(
            src_ref=sent.at[r],
            dst_ref=arrived.at[r],
            send_sem=tone_send.at[r],
            recv_sem=tone_recv.at[r],
            device_id=partner,
            device_id_type=pl.DeviceIdType.MESH,
        )
        passing.start()
        passing.wait()
        running = running + arrived[r]
    tones_ref[...] = running * scale
    finish(0)
    finish(1)


def exchange(zero, blocks, halo, delays, valid, tone_chan, tables, sizes, scale):
    n = math.prod(sizes)
    rounds = (sizes[1] * sizes[2]).bit_length() - 1
    stations = blocks.shape[0]
    whole = lambda shape: pl.BlockSpec(shape, lambda i: (0,) * len(shape))
    smem = pl.BlockSpec(memory_space=pltpu.SMEM)
    return pl.pallas_call(
        lambda *refs: exchange_kernel(sizes, scale, *refs),
        out_shape=(
            jax.ShapeDtypeStruct((2, n, 2, FA, LANES), jnp.bfloat16),
            jax.ShapeDtypeStruct((NTONE, LANES), jnp.float32),
        ),
        grid=(1,),
        in_specs=[
            pl.BlockSpec(memory_space=pl.ANY),
            smem,
            smem,
            smem,
            pl.BlockSpec((stations, 2 * FA, LANES), lambda i: (0, 1, 0)),
            whole((stations, FA, LANES)),
            whole((2 * FA, FA)),
            whole((FA, FB)),
            whole((FA, FB)),
            whole((FB // 2, 2 * FB)),
        ],
        out_specs=(pl.BlockSpec(memory_space=pl.ANY), whole((NTONE, LANES))),
        scratch_shapes=STAGE_SCRATCH
        + [
            pltpu.VMEM((FB // 2, FA, LANES), jnp.bfloat16),
            pltpu.VMEM((NTONE, LANES), jnp.float32),
            pltpu.VMEM((rounds, NTONE, LANES), jnp.float32),
            pltpu.VMEM((rounds, NTONE, LANES), jnp.float32),
            pltpu.SemaphoreType.DMA((2,)),
            pltpu.SemaphoreType.DMA((2, n)),
            pltpu.SemaphoreType.DMA((2, n)),
            pltpu.SemaphoreType.DMA,
            pltpu.SemaphoreType.DMA((rounds,)),
            pltpu.SemaphoreType.DMA((rounds,)),
        ],
        compiler_params=pltpu.CompilerParams(
            collective_id=0, has_side_effects=True, vmem_limit_bytes=VMEM_LIMIT
        ),
    )(zero, delays, valid, tone_chan, blocks, halo, *tables)


CB = 64


def correlate_kernel(scale, got_ref, out_ref, matrix, power, turned):
    lane = lax.broadcasted_iota(jnp.int32, (CB, LANES), 1)
    low = lane % 64 < 32
    n_time = got_ref.shape[2]
    rows = 4 * n_time
    pitch = rows + 1
    for u in range(2):
        for j in range(n_time):
            y0 = got_ref[u, 0, j].astype(jnp.float32)
            y1 = got_ref[u, 1, j].astype(jnp.float32)
            t = (u * n_time + j) * 2
            matrix[pl.ds(t, CB, stride=pitch), :] = jnp.where(low, y0, pltpu.roll(y1, 32, 1))
            matrix[pl.ds(t + 1, CB, stride=pitch), :] = jnp.where(low, pltpu.roll(y0, 96, 1), y1)
    left = lax.broadcasted_iota(jnp.int32, (S, LANES), 1) < 64
    left_half = lax.broadcasted_iota(jnp.int32, (S // 2, LANES), 1) < 64

    def channel(c, carry):
        values = matrix[pl.ds(c * pitch, rows), :].astype(jnp.bfloat16)
        gram = lax.dot_general(
            values, values, (((0,), (0,)), ((), ())), preferred_element_type=jnp.float32
        )
        upper = gram[:S] * scale
        lower = pltpu.roll(gram[S:] * scale, 64, 1)
        slot = pl.multiple_of((c % 8) * S, S)
        power[pl.ds(slot, S), :] = jnp.where(left, upper + lower, lower - upper)
        even = power[pl.ds(slot, S // 2, stride=2), :]
        odd = power[pl.ds(slot + 1, S // 2, stride=2), :]
        turned[pl.ds(c, S // 2, stride=CB + 1), :] = jnp.where(left_half, even, pltpu.roll(odd, 64, 1))
        turned[pl.ds(S // 2 * (CB + 1) + c, S // 2, stride=CB + 1), :] = jnp.where(
            left_half, pltpu.roll(even, 64, 1), odd
        )
        return carry

    lax.fori_loop(0, CB, channel, 0, unroll=8)
    for tile in range(S):
        at = tile * (CB + 1)
        out_ref[:, tile * LANES : (tile + 1) * LANES] = turned[at : at + CB, :]


def correlate(got, scale):
    _, n_stn, n_time, channels, _ = got.shape
    return pl.pallas_call(
        lambda *refs: correlate_kernel(scale, *refs),
        out_shape=jax.ShapeDtypeStruct((channels, 2 * S * S), jnp.float32),
        grid=(channels // CB,),
        in_specs=[pl.BlockSpec((2, n_stn, n_time, CB, LANES), lambda i: (0, 0, 0, i, 0))],
        out_specs=pl.BlockSpec((CB, 2 * S * S), lambda i: (i, 0)),
        scratch_shapes=[
            pltpu.VMEM((CB * (4 * n_time + 1), LANES), jnp.float32),
            pltpu.VMEM((8 * S, LANES), jnp.float32),
            pltpu.VMEM((S * (CB + 1), LANES), jnp.float32),
        ],
        compiler_params=pltpu.CompilerParams(vmem_limit_bytes=VMEM_LIMIT),
        cost_estimate=pl.CostEstimate(
            flops=2 * channels * 64 * 128 * 128, bytes_accessed=26 * 2**20, transcendentals=0
        ),
    )(got)


def fast_shards(samples, delays, valid, tone_chan):
    tables = fast_tables()
    sizes = tuple(lax.axis_size(name) for name in ("stn", "tm", "cores"))
    n_stn, n_tm, n_cores = sizes
    stations, stretch = samples.shape
    trailing = passed_along(samples[:, :MAXD], ("tm", "cores"), -1)
    blocks = samples.reshape(stations, stretch // LANES, LANES)
    zero = channelize_pair(0, blocks, (blocks, 2), delays, valid, tables)
    halo = trailing.reshape(stations, MAXD // LANES, LANES)
    channels = NCH // math.prod(sizes)
    scale = 1.0 / math.sqrt(stretch // (FA * FB) * n_tm * n_cores)
    got, picks = exchange(zero, blocks, halo, delays, valid, tone_chan, tables, sizes, scale)
    got = got.reshape(2, n_stn, n_tm * n_cores, channels, LANES)
    visibility = correlate(got, scale)
    mine = picks.reshape(NTONE, 2, 2, stations)[:, :, 0]
    phase_cal = jnp.transpose(mine, (2, 1, 0)).reshape(stations, 2 * NTONE)
    return (visibility, phase_cal)


def solution(mesh):
    sizes = mesh.shape
    body = fast_shards if sizes["stn"] == 2 and math.prod(sizes.values()) == 32 else shards
    return jax.shard_map(
        body,
        mesh=mesh,
        in_specs=(P("stn", ("tm", "cores")), P("stn"), P("stn"), P("stn", None)),
        out_specs=(P(("stn", "tm", "cores"), None), P("stn", None)),
        check_vma=False,
    )
```

profile of v0, /device:TPU:0, one launch (start us, length us, event | category | flops | bytes accessed | tf_op | source)
XLA Modules:
  0.0 298.2 jit_solution(15767174018166562224)
XLA Ops:
  0.6 1.7 slice.6
  2.4 1.3 collective-permute-start
  3.7 8.8 %copy.14 = bf16[4,8,1024,128]{3,2,1,0:T(8,128)(2,1)} copy(bf16[4,8,1024,128]{3,1,2,0:T(8,128)(2,1)} %bitcast.13) | data formatting | bytes 16777216
  12.4 33.9 %shard_map.95.refs_0_ = bf16[64,256,128]{2,1,0:T(8,128)(2,1)} custom-call(s32[32]{0:T(128)} %refs_1_.1, s32[32]{0:T(128)} %refs_2_.1, bf16[32,1024,128]{2,1,0:T(8,128)(2,1)} %bitcast.10, bf16[32,1024,128]{2,1,0:T(8,128)(2,1)} %bitcast.11, bf16[512,256]{1,0:T(8,128)(2,1)} %constant.8.clone.one_ref.refs_6_, f32[256,128]{1,0:T(8,128)} %constant.9.clone.cos_ref.refs_7_, ...), custom_call_target="tpu_custom_call" | custom-call | flops 6442450944 | bytes 10485760 | tf_op jit(solution)/shard_map/pallas_call | solution.py:209
  46.4 6.5 %collective-permute-done = bf16[32,32768]{1,0:T(8,128)(2,1)S(1)} collective-permute-done((bf16[32,32768]{1,0:T(8,128)(2,1)S(1)}, bf16[32,32768]{1,0:T(8,128)(2,1)S(1)}, u32[]{:S(2)}, u32[]{:S(2)}) %collective-permute-start) | collective-permute-done | bytes 2097184 | tf_op jit(solution)/shard_map/ppermute | solution.py:23
  52.8 1.8 copy.15
  54.6 206.3 %shard_map.96 = (bf16[2,32,2,256,128]{4,3,2,1,0:T(8,128)(2,1)}, f32[64,128]{1,0:T(8,128)}) custom-call(bf16[64,256,128]{2,1,0:T(8,128)(2,1)} %shard_map.95.refs_0_, s32[32]{0:T(128)} %refs_1_.1, s32[32]{0:T(128)} %refs_2_.1, s32[32,64]{1,0:T(8,128)} %refs_3_.1, bf16[32,1024,128]{2,1,0:T(8,128)(2,1)} %bitcast.12, bf16[32,256,128]{2,1,0:T(8,128)(2,1)} %bitcast.15, ...), custom_call_target="tpu_custom_call" | custom-call | tf_op jit(solution)/shard_map/pallas_call | solution.py:357
  260.9 0.8 copy.12
  261.8 0.7 reshape.23
  262.5 35.6 %shard_map.97 = f32[512,8192]{1,0:T(8,128)} custom-call(bf16[2,2,16,512,128]{4,3,2,1,0:T(8,128)(2,1)} %bitcast.14), custom_call_target="tpu_custom_call" | custom-call | flops 1073741824 | bytes 27262976 | tf_op jit(solution)/shard_map/pallas_call | solution.py:440
  (2 shorter events, 0.0 us)
Async XLA Ops:
  2.4 50.5 %collective-permute-start = (bf16[32,32768]{1,0:T(8,128)(2,1)S(1)}, bf16[32,32768]{1,0:T(8,128)(2,1)S(1)}, u32[]{:S(2)}, u32[]{:S(2)}) collective-permute-start(bf16[32,32768]{1,0:T(8,128)(2,1)S(1)} %slice.6), channel_id=1, source_target_pairs={{1,0},{2,1},{3,2},{4,3},{5,4},{6,5},{7,6},{8,7},{9,8},{10,9},{11,1... | collective-permute-start | bytes 6291464 | tf_op jit(solution)/shard_map/ppermute | solution.py:23
where the time goes:
time: 299 us; the launch traced here: 298 us
  Pallas kernels  276 us (92%)
  local copies, waits for them, and re-layouts  13.9 us (5%)
  waiting for transfers between devices  6.46 us (2%)
    pallas_call x1, Pallas kernels, exchange(): pl.pallas_call(lambda *refs: exchange_kernel(sizes, scale, *refs), out_sh...  206 us
    pallas_call x1, Pallas kernels, correlate(): pl.pallas_call(lambda *refs: correlate_kernel(scale, *refs), out_shape=ja...  35.6 us
    pallas_call x1, Pallas kernels, channelize_pair(): pl.pallas_call(channelize_kernel, out_shape=jax.ShapeDtypeStruct((FB // 2...  33.9 us
    unnamed x2, local copies, waits for them, and re-layouts  10.6 us
    ppermute x1, waiting for transfers between devices, passed_along(): return lax.ppermute(block, axis, route)  6.46 us
  transfers between devices with their start and end apart: 1, of which 1 were waited for; matrix products, arithmetic and copies ran while one was open for 3% of the time, Pallas kernels for 11%

commit v1 on v0

--- a/solution.py
+++ b/solution.py
@@ -250,37 +250,51 @@
     lax.fori_loop(0, NTONE, tone, 0)
 
 
-def exchange_kernel(sizes, scale, zero_ref, delay_ref, valid_ref, tone_ref, main_ref, next_ref, one_ref,
+def exchange_kernel(sizes, scale, zero_ref, delay_ref, valid_ref, tone_ref, blocks_ref, halo_ref, one_ref,
                     cos_ref, sin_ref, two_ref, got_ref, tones_ref, stream, twist_re, twist_im,
-                    turned, later, picks, sent, arrived, local_sem, send_sem, recv_sem, load_sem,
+                    turned, later, main_ref, next_ref, picks, sent, arrived, local_sem, send_sem, recv_sem, load_sem,
                     tone_send, tone_recv):
     _, n_tm, n_cores = sizes
     n = math.prod(sizes)
     me = linear_index(sizes)
 
-    def place(device):
-        return (device // (n_tm * n_cores), (device // n_cores) % n_tm, device % n_cores)
+    self_at = 4
+
+    def place(i):
+        turn = (i + i // n_tm) % 4
+        return (
+            (lax.axis_index("stn") + turn // 2) % 2,
+            (lax.axis_index("tm") + 3 * i + 4) % n_tm,
+            (lax.axis_index("cores") + turn) % 2,
+        )
+
+    def others(body):
+        def step(i, carry):
+            body(i)
+            return carry
+
+        lax.fori_loop(0, self_at, step, 0)
+        lax.fori_loop(self_at + 1, n, step, 0)
 
     barrier = pltpu.get_barrier_semaphore()
 
-    def greet(k, carry):
-        pl.semaphore_signal(
-            barrier, inc=1, device_id=place((me + k) % n), device_id_type=pl.DeviceIdType.MESH
-        )
-        return carry
-
-    lax.fori_loop(1, n, greet, 0)
+    others(
+        lambda i: pl.semaphore_signal(
+            barrier, inc=1, device_id=place(i), device_id_type=pl.DeviceIdType.MESH
+        )
+    )
     pl.semaphore_wait(barrier, n - 1)
     sources = (zero_ref, later)
 
     def copy(pair, k):
-        to = (me + k) % n
+        where = place(k)
+        to = (where[0] * n_tm + where[1]) * n_cores + where[2]
         return pltpu.make_async_remote_copy(
             src_ref=sources[pair].at[pl.ds(to * 2, 2)],
             dst_ref=got_ref.at[pair, me],
             send_sem=send_sem.at[pair, k],
             recv_sem=recv_sem.at[pair, k],
-            device_id=place(to),
+            device_id=where,
             device_id_type=pl.DeviceIdType.MESH,
         )
 
@@ -290,17 +304,22 @@
         )
 
     def send(pair):
-        lax.fori_loop(1, n, lambda k, carry: (copy(pair, k).start(), carry)[1], 0)
+        others(lambda i: copy(pair, i).start())
         own(pair).start()
 
     def finish(pair):
         own(pair).wait()
-        lax.fori_loop(1, n, lambda k, carry: (copy(pair, k).wait(), carry)[1], 0)
+        others(lambda i: copy(pair, i).wait())
 
     send(0)
-    load = pltpu.make_async_copy(zero_ref, later, load_sem)
-    load.start()
-    load.wait()
+    loads = [
+        pltpu.make_async_copy(zero_ref, later, load_sem.at[0]),
+        pltpu.make_async_copy(blocks_ref.at[:, pl.ds(2 * FA, 2 * FA)], main_ref, load_sem.at[1]),
+        pltpu.make_async_copy(halo_ref, next_ref, load_sem.at[2]),
+    ]
+    for load in loads:
+        load.start()
+    loads[0].wait()
 
     def widen(q, carry):
         turned[pl.ds(q * (FA + 1), FA), :] = later[q].astype(jnp.float32)
@@ -318,6 +337,8 @@
                     stream, twist_re, twist_im)
         return carry
 
+    loads[1].wait()
+    loads[2].wait()
     lax.fori_loop(0, stations, station, 0)
     second_stage(two_ref, later, twist_re, twist_im, turned)
     send(1)
@@ -366,8 +387,8 @@
             smem,
             smem,
             smem,
-            pl.BlockSpec((stations, 2 * FA, LANES), lambda i: (0, 1, 0)),
-            whole((stations, FA, LANES)),
+            pl.BlockSpec(memory_space=pl.ANY),
+            pl.BlockSpec(memory_space=pl.ANY),
             whole((2 * FA, FA)),
             whole((FA, FB)),
             whole((FA, FB)),
@@ -377,13 +398,15 @@
         scratch_shapes=STAGE_SCRATCH
         + [
             pltpu.VMEM((FB // 2, FA, LANES), jnp.bfloat16),
+            pltpu.VMEM((stations, 2 * FA, LANES), jnp.bfloat16),
+            pltpu.VMEM((stations, FA, LANES), jnp.bfloat16),
             pltpu.VMEM((NTONE, LANES), jnp.float32),
             pltpu.VMEM((rounds, NTONE, LANES), jnp.float32),
             pltpu.VMEM((rounds, NTONE, LANES), jnp.float32),
             pltpu.SemaphoreType.DMA((2,)),
             pltpu.SemaphoreType.DMA((2, n)),
             pltpu.SemaphoreType.DMA((2, n)),
-            pltpu.SemaphoreType.DMA,
+            pltpu.SemaphoreType.DMA((3,)),
             pltpu.SemaphoreType.DMA((rounds,)),
             pltpu.SemaphoreType.DMA((rounds,)),
         ],

time: 299 us -> 286 us (0.957)
  Pallas kernels: 276 us -> 262 us
    pallas_call x1, Pallas kernels: 206 us -> 193 us  [exchange(): pl.pallas_call(lambda *refs: exchange_kernel(sizes, scale, *refs), out_sh...]
  transfers between devices with their start and end apart: 1 -> 1, of which waited for: 1 -> 1; matrix products, arithmetic and copies ran while one was open for 3% -> 3% of each run, Pallas kernels for 11% -> 12%
where the time goes in v1:
time: 286 us; the launch traced here: 285 us
  Pallas kernels  262 us (92%)
  local copies, waits for them, and re-layouts  13.9 us (5%)
  waiting for transfers between devices  6.46 us (2%)
    pallas_call x1, Pallas kernels, exchange(): pl.pallas_call(lambda *refs: exchange_kernel(sizes, scale, *refs), out_sh...  193 us
    pallas_call x1, Pallas kernels, correlate(): pl.pallas_call(lambda *refs: correlate_kernel(scale, *refs), out_shape=ja...  35.6 us
    pallas_call x1, Pallas kernels, channelize_pair(): pl.pallas_call(channelize_kernel, out_shape=jax.ShapeDtypeStruct((FB // 2...  33.9 us
    unnamed x2, local copies, waits for them, and re-layouts  10.6 us
    ppermute x1, waiting for transfers between devices, passed_along(): return lax.ppermute(block, axis, route)  6.46 us
  transfers between devices with their start and end apart: 1, of which 1 were waited for; matrix products, arithmetic and copies ran while one was open for 3% of the time, Pallas kernels for 12%

profile of v1, /device:TPU:0, one launch (start us, length us, event | category | flops | bytes accessed | tf_op | source)
XLA Modules:
  0.0 284.8 jit_solution(1688031929424464565)
XLA Ops:
  0.6 1.7 slice.6
  2.4 1.3 collective-permute-start
  3.7 8.8 %copy.14 = bf16[4,8,1024,128]{3,2,1,0:T(8,128)(2,1)} copy(bf16[4,8,1024,128]{3,1,2,0:T(8,128)(2,1)} %bitcast.13) | data formatting | bytes 16777216
  12.4 33.9 %shard_map.95.refs_0_ = bf16[64,256,128]{2,1,0:T(8,128)(2,1)} custom-call(s32[32]{0:T(128)} %refs_1_.1, s32[32]{0:T(128)} %refs_2_.1, bf16[32,1024,128]{2,1,0:T(8,128)(2,1)} %bitcast.10, bf16[32,1024,128]{2,1,0:T(8,128)(2,1)} %bitcast.11, bf16[512,256]{1,0:T(8,128)(2,1)} %constant.8.clone.one_ref.refs_6_, f32[256,128]{1,0:T(8,128)} %constant.9.clone.cos_ref.refs_7_, ...), custom_call_target="tpu_custom_call" | custom-call | flops 6442450944 | bytes 10485760 | tf_op jit(solution)/shard_map/pallas_call | solution.py:209
  46.4 6.5 %collective-permute-done = bf16[32,32768]{1,0:T(8,128)(2,1)S(1)} collective-permute-done((bf16[32,32768]{1,0:T(8,128)(2,1)S(1)}, bf16[32,32768]{1,0:T(8,128)(2,1)S(1)}, u32[]{:S(2)}, u32[]{:S(2)}) %collective-permute-start) | collective-permute-done | bytes 2097184 | tf_op jit(solution)/shard_map/ppermute | solution.py:23
  52.8 1.8 copy.15
  54.6 192.9 %shard_map.96 = (bf16[2,32,2,256,128]{4,3,2,1,0:T(8,128)(2,1)}, f32[64,128]{1,0:T(8,128)}) custom-call(bf16[64,256,128]{2,1,0:T(8,128)(2,1)} %shard_map.95.refs_0_, s32[32]{0:T(128)} %refs_1_.1, s32[32]{0:T(128)} %refs_2_.1, s32[32,64]{1,0:T(8,128)} %refs_3_.1, bf16[32,1024,128]{2,1,0:T(8,128)(2,1)} %bitcast.12, bf16[32,256,128]{2,1,0:T(8,128)(2,1)} %bitcast.15, ...), custom_call_target="tpu_custom_call" | custom-call | tf_op jit(solution)/shard_map/pallas_call | solution.py:378
  247.6 0.8 copy.12
  248.5 0.7 reshape.23
  249.2 35.6 %shard_map.97 = f32[512,8192]{1,0:T(8,128)} custom-call(bf16[2,2,16,512,128]{4,3,2,1,0:T(8,128)(2,1)} %bitcast.14), custom_call_target="tpu_custom_call" | custom-call | flops 1073741824 | bytes 27262976 | tf_op jit(solution)/shard_map/pallas_call | solution.py:463
  (2 shorter events, 0.0 us)
Async XLA Ops:
  2.4 50.5 %collective-permute-start = (bf16[32,32768]{1,0:T(8,128)(2,1)S(1)}, bf16[32,32768]{1,0:T(8,128)(2,1)S(1)}, u32[]{:S(2)}, u32[]{:S(2)}) collective-permute-start(bf16[32,32768]{1,0:T(8,128)(2,1)S(1)} %slice.6), channel_id=1, source_target_pairs={{1,0},{2,1},{3,2},{4,3},{5,4},{6,5},{7,6},{8,7},{9,8},{10,9},{11,1... | collective-permute-start | bytes 6291464 | tf_op jit(solution)/shard_map/ppermute | solution.py:23

commit v2 on v1

--- a/solution.py
+++ b/solution.py
@@ -170,7 +170,7 @@
         turned[pl.ds(k, FB // 2, stride=FA + 1), :] = product
         return carry
 
-    lax.fori_loop(0, FA, second, 0, unroll=8)
+    lax.fori_loop(0, FA, second, 0, unroll=16)
 
     def write(q, carry):
         out_ref[q] = turned[pl.ds(q * (FA + 1), FA), :].astype(jnp.bfloat16)
@@ -180,6 +180,7 @@
 
 
 PITCH = 65
+TOGETHER = 4
 STAGE_SCRATCH = [
     pltpu.VMEM((3 * FA + 8, LANES), jnp.float32),
     pltpu.VMEM((FA * PITCH + 7, LANES), jnp.float32),
@@ -190,14 +191,16 @@
 
 def channelize_kernel(delay_ref, valid_ref, main_ref, next_ref, one_ref, cos_ref, sin_ref, two_ref,
                       out_ref, stream, twist_re, twist_im, turned):
-    s = pl.program_id(0)
     rows = 2 * FA
-    stream[0:rows, :] = main_ref[0].astype(jnp.float32)
-    stream[rows : rows + FA, :] = next_ref[0].astype(jnp.float32)
-    first_stage(s, delay_ref[s], valid_ref[s].astype(jnp.float32), one_ref, cos_ref, sin_ref,
-                stream, twist_re, twist_im)
-
-    @pl.when(s == pl.num_programs(0) - 1)
+    for i in range(TOGETHER):
+        stream[i, 0:rows, :] = main_ref[i].astype(jnp.float32)
+        stream[i, rows : rows + FA, :] = next_ref[i].astype(jnp.float32)
+    for i in range(TOGETHER):
+        s = pl.program_id(0) * TOGETHER + i
+        first_stage(s, delay_ref[s], valid_ref[s].astype(jnp.float32), one_ref, cos_ref, sin_ref,
+                    stream.at[i], twist_re, twist_im)
+
+    @pl.when(pl.program_id(0) == pl.num_programs(0) - 1)
     def _():
         second_stage(two_ref, out_ref, twist_re, twist_im, turned)
 
@@ -211,17 +214,17 @@
         out_shape=jax.ShapeDtypeStruct((FB // 2, FA, LANES), jnp.bfloat16),
         grid_spec=pltpu.PrefetchScalarGridSpec(
             num_scalar_prefetch=2,
-            grid=(blocks.shape[0],),
+            grid=(blocks.shape[0] // TOGETHER,),
             in_specs=[
-                pl.BlockSpec((1, 2 * FA, LANES), lambda s, *_: (s, pair, 0)),
-                pl.BlockSpec((1, FA, LANES), lambda s, *_: (s, next_at, 0)),
+                pl.BlockSpec((TOGETHER, 2 * FA, LANES), lambda s, *_: (s, pair, 0)),
+                pl.BlockSpec((TOGETHER, FA, LANES), lambda s, *_: (s, next_at, 0)),
                 whole((2 * FA, FA)),
                 whole((FA, FB)),
                 whole((FA, FB)),
                 whole((FB // 2, 2 * FB)),
             ],
             out_specs=whole((FB // 2, FA, LANES)),
-            scratch_shapes=STAGE_SCRATCH,
+            scratch_shapes=[pltpu.VMEM((TOGETHER, 3 * FA + 8, LANES), jnp.float32)] + STAGE_SCRATCH[1:],
         ),
         compiler_params=pltpu.CompilerParams(vmem_limit_bytes=VMEM_LIMIT),
         cost_estimate=pl.CostEstimate(
@@ -442,7 +445,7 @@
         )
         upper = gram[:S] * scale
         lower = pltpu.roll(gram[S:] * scale, 64, 1)
-        slot = pl.multiple_of((c % 8) * S, S)
+        slot = pl.multiple_of((c % 16) * S, S)
         power[pl.ds(slot, S), :] = jnp.where(left, upper + lower, lower - upper)
         even = power[pl.ds(slot, S // 2, stride=2), :]
         odd = power[pl.ds(slot + 1, S // 2, stride=2), :]
@@ -452,7 +455,7 @@
         )
         return carry
 
-    lax.fori_loop(0, CB, channel, 0, unroll=8)
+    lax.fori_loop(0, CB, channel, 0, unroll=16)
     for tile in range(S):
         at = tile * (CB + 1)
         out_ref[:, tile * LANES : (tile + 1) * LANES] = turned[at : at + CB, :]
@@ -468,7 +471,7 @@
         out_specs=pl.BlockSpec((CB, 2 * S * S), lambda i: (i, 0)),
         scratch_shapes=[
             pltpu.VMEM((CB * (4 * n_time + 1), LANES), jnp.float32),
-            pltpu.VMEM((8 * S, LANES), jnp.float32),
+            pltpu.VMEM((16 * S, LANES), jnp.float32),
             pltpu.VMEM((S * (CB + 1), LANES), jnp.float32),
         ],
         compiler_params=pltpu.CompilerParams(vmem_limit_bytes=VMEM_LIMIT),

time: 286 us -> 299 us (1.045)
  waiting for transfers between devices: 6.46 us -> 20.4 us
    pallas_call x1, Pallas kernels: 35.6 us -> 49.6 us  [correlate(): pl.pallas_call(lambda *refs: correlate_kernel(scale, *refs), out_shape=ja...]
    ppermute x1, waiting for transfers between devices: 6.46 us -> 20.4 us  [passed_along(): return lax.ppermute(block, axis, route)]
    pallas_call x1, Pallas kernels: 33.9 us -> 20 us  [channelize_pair(): pl.pallas_call(channelize_kernel, out_shape=jax.ShapeDtypeStruct((FB // 2...]
  transfers between devices with their start and end apart: 1 -> 1, of which waited for: 1 -> 1; matrix products, arithmetic and copies ran while one was open for 3% -> 3% of each run, Pallas kernels for 12% -> 7%
where the time goes in v2:
time: 299 us
  Pallas kernels  262 us (88%)
  waiting for transfers between devices  20.4 us (7%)
  local copies, waits for them, and re-layouts  13.9 us (5%)
    pallas_call x1, Pallas kernels, exchange(): pl.pallas_call(lambda *refs: exchange_kernel(sizes, scale, *refs), out_sh...  193 us
    pallas_call x1, Pallas kernels, correlate(): pl.pallas_call(lambda *refs: correlate_kernel(scale, *refs), out_shape=ja...  49.6 us
    ppermute x1, waiting for transfers between devices, passed_along(): return lax.ppermute(block, axis, route)  20.4 us
    pallas_call x1, Pallas kernels, channelize_pair(): pl.pallas_call(channelize_kernel, out_shape=jax.ShapeDtypeStruct((FB // 2...  20 us
    unnamed x2, local copies, waits for them, and re-layouts  10.6 us
  transfers between devices with their start and end apart: 1, of which 1 were waited for; matrix products, arithmetic and copies ran while one was open for 3% of the time, Pallas kernels for 7%

profile of v2, /device:TPU:0, one launch (start us, length us, event | category | flops | bytes accessed | tf_op | source)
XLA Modules:
  0.0 298.7 jit_solution(9101715489279755425)
XLA Ops:
  0.6 1.7 slice.6
  2.4 1.3 collective-permute-start
  3.7 8.8 %copy.14 = bf16[4,8,1024,128]{3,2,1,0:T(8,128)(2,1)} copy(bf16[4,8,1024,128]{3,1,2,0:T(8,128)(2,1)} %bitcast.13) | data formatting | bytes 16777216
  12.4 20.0 %shard_map.95.refs_0_ = bf16[64,256,128]{2,1,0:T(8,128)(2,1)} custom-call(s32[32]{0:T(128)} %refs_1_.1, s32[32]{0:T(128)} %refs_2_.1, bf16[32,1024,128]{2,1,0:T(8,128)(2,1)} %bitcast.10, bf16[32,1024,128]{2,1,0:T(8,128)(2,1)} %bitcast.11, bf16[512,256]{1,0:T(8,128)(2,1)} %constant.8.clone.one_ref.refs_6_, f32[256,128]{1,0:T(8,128)} %constant.9.clone.cos_ref.refs_7_, ...), custom_call_target="tpu_custom_call" | custom-call | flops 6442450944 | bytes 10485760 | tf_op jit(solution)/shard_map/pallas_call | solution.py:212
  32.5 20.4 %collective-permute-done = bf16[32,32768]{1,0:T(8,128)(2,1)S(1)} collective-permute-done((bf16[32,32768]{1,0:T(8,128)(2,1)S(1)}, bf16[32,32768]{1,0:T(8,128)(2,1)S(1)}, u32[]{:S(2)}, u32[]{:S(2)}) %collective-permute-start) | collective-permute-done | bytes 2097184 | tf_op jit(solution)/shard_map/ppermute | solution.py:23
  52.8 1.8 copy.15
  54.6 192.8 %shard_map.96 = (bf16[2,32,2,256,128]{4,3,2,1,0:T(8,128)(2,1)}, f32[64,128]{1,0:T(8,128)}) custom-call(bf16[64,256,128]{2,1,0:T(8,128)(2,1)} %shard_map.95.refs_0_, s32[32]{0:T(128)} %refs_1_.1, s32[32]{0:T(128)} %refs_2_.1, s32[32,64]{1,0:T(8,128)} %refs_3_.1, bf16[32,1024,128]{2,1,0:T(8,128)(2,1)} %bitcast.12, bf16[32,256,128]{2,1,0:T(8,128)(2,1)} %bitcast.15, ...), custom_call_target="tpu_custom_call" | custom-call | tf_op jit(solution)/shard_map/pallas_call | solution.py:381
  247.5 0.8 copy.12
  248.4 0.7 reshape.23
  249.0 49.6 %shard_map.97 = f32[512,8192]{1,0:T(8,128)} custom-call(bf16[2,2,16,512,128]{4,3,2,1,0:T(8,128)(2,1)} %bitcast.14), custom_call_target="tpu_custom_call" | custom-call | flops 1073741824 | bytes 27262976 | tf_op jit(solution)/shard_map/pallas_call | solution.py:466
  (2 shorter events, 0.0 us)
Async XLA Ops:
  2.4 50.5 %collective-permute-start = (bf16[32,32768]{1,0:T(8,128)(2,1)S(1)}, bf16[32,32768]{1,0:T(8,128)(2,1)S(1)}, u32[]{:S(2)}, u32[]{:S(2)}) collective-permute-start(bf16[32,32768]{1,0:T(8,128)(2,1)S(1)} %slice.6), channel_id=1, source_target_pairs={{1,0},{2,1},{3,2},{4,3},{5,4},{6,5},{7,6},{8,7},{9,8},{10,9},{11,1... | collective-permute-start | bytes 6291464 | tf_op jit(solution)/shard_map/ppermute | solution.py:23

commit v3 on v2

--- a/solution.py
+++ b/solution.py
@@ -455,7 +455,7 @@
         )
         return carry
 
-    lax.fori_loop(0, CB, channel, 0, unroll=16)
+    lax.fori_loop(0, CB, channel, 0, unroll=4)
     for tile in range(S):
         at = tile * (CB + 1)
         out_ref[:, tile * LANES : (tile + 1) * LANES] = turned[at : at + CB, :]

time: 299 us -> 306 us (1.023)
  Pallas kernels: 262 us -> 269 us
    pallas_call x1, Pallas kernels: 49.6 us -> 56.2 us  [correlate(): pl.pallas_call(lambda *refs: correlate_kernel(scale, *refs), out_shape=ja...]
where the time goes in v3:
time: 306 us; the launch traced here: 305 us
  Pallas kernels  269 us (88%)
  waiting for transfers between devices  20.4 us (7%)
  local copies, waits for them, and re-layouts  13.9 us (5%)
    pallas_call x1, Pallas kernels, exchange(): pl.pallas_call(lambda *refs: exchange_kernel(sizes, scale, *refs), out_sh...  193 us
    pallas_call x1, Pallas kernels, correlate(): pl.pallas_call(lambda *refs: correlate_kernel(scale, *refs), out_shape=ja...  56.2 us
    ppermute x1, waiting for transfers between devices, passed_along(): return lax.ppermute(block, axis, route)  20.4 us
    pallas_call x1, Pallas kernels, channelize_pair(): pl.pallas_call(channelize_kernel, out_shape=jax.ShapeDtypeStruct((FB // 2...  20 us
    unnamed x2, local copies, waits for them, and re-layouts  10.6 us
  transfers between devices with their start and end apart: 1, of which 1 were waited for; matrix products, arithmetic and copies ran while one was open for 3% of the time, Pallas kernels for 7%

profile of v3, /device:TPU:0, one launch (start us, length us, event | category | flops | bytes accessed | tf_op | source)
XLA Modules:
  0.0 305.3 jit_solution(13990753044701480678)
XLA Ops:
  0.6 1.7 slice.6
  2.4 1.3 collective-permute-start
  3.7 8.8 %copy.14 = bf16[4,8,1024,128]{3,2,1,0:T(8,128)(2,1)} copy(bf16[4,8,1024,128]{3,1,2,0:T(8,128)(2,1)} %bitcast.13) | data formatting | bytes 16777216
  12.4 20.0 %shard_map.95.refs_0_ = bf16[64,256,128]{2,1,0:T(8,128)(2,1)} custom-call(s32[32]{0:T(128)} %refs_1_.1, s32[32]{0:T(128)} %refs_2_.1, bf16[32,1024,128]{2,1,0:T(8,128)(2,1)} %bitcast.10, bf16[32,1024,128]{2,1,0:T(8,128)(2,1)} %bitcast.11, bf16[512,256]{1,0:T(8,128)(2,1)} %constant.8.clone.one_ref.refs_6_, f32[256,128]{1,0:T(8,128)} %constant.9.clone.cos_ref.refs_7_, ...), custom_call_target="tpu_custom_call" | custom-call | flops 6442450944 | bytes 10485760 | tf_op jit(solution)/shard_map/pallas_call | solution.py:212
  32.5 20.4 %collective-permute-done = bf16[32,32768]{1,0:T(8,128)(2,1)S(1)} collective-permute-done((bf16[32,32768]{1,0:T(8,128)(2,1)S(1)}, bf16[32,32768]{1,0:T(8,128)(2,1)S(1)}, u32[]{:S(2)}, u32[]{:S(2)}) %collective-permute-start) | collective-permute-done | bytes 2097184 | tf_op jit(solution)/shard_map/ppermute | solution.py:23
  52.8 1.8 copy.15
  54.6 192.8 %shard_map.96 = (bf16[2,32,2,256,128]{4,3,2,1,0:T(8,128)(2,1)}, f32[64,128]{1,0:T(8,128)}) custom-call(bf16[64,256,128]{2,1,0:T(8,128)(2,1)} %shard_map.95.refs_0_, s32[32]{0:T(128)} %refs_1_.1, s32[32]{0:T(128)} %refs_2_.1, s32[32,64]{1,0:T(8,128)} %refs_3_.1, bf16[32,1024,128]{2,1,0:T(8,128)(2,1)} %bitcast.12, bf16[32,256,128]{2,1,0:T(8,128)(2,1)} %bitcast.15, ...), custom_call_target="tpu_custom_call" | custom-call | tf_op jit(solution)/shard_map/pallas_call | solution.py:381
  247.5 0.8 copy.12
  248.4 0.7 reshape.23
  249.0 56.2 %shard_map.97 = f32[512,8192]{1,0:T(8,128)} custom-call(bf16[2,2,16,512,128]{4,3,2,1,0:T(8,128)(2,1)} %bitcast.14), custom_call_target="tpu_custom_call" | custom-call | flops 1073741824 | bytes 27262976 | tf_op jit(solution)/shard_map/pallas_call | solution.py:466
  (2 shorter events, 0.0 us)
Async XLA Ops:
  2.4 50.5 %collective-permute-start = (bf16[32,32768]{1,0:T(8,128)(2,1)S(1)}, bf16[32,32768]{1,0:T(8,128)(2,1)S(1)}, u32[]{:S(2)}, u32[]{:S(2)}) collective-permute-start(bf16[32,32768]{1,0:T(8,128)(2,1)S(1)} %slice.6), channel_id=1, source_target_pairs={{1,0},{2,1},{3,2},{4,3},{5,4},{6,5},{7,6},{8,7},{9,8},{10,9},{11,1... | collective-permute-start | bytes 6291464 | tf_op jit(solution)/shard_map/ppermute | solution.py:23
